TPU v7x, 256 devices: a whole 4x4x8 slice. The times are simulated.
256 devices in a mesh: dp: 64 (over z, y, x_lo), mp: 4 (over x_hi, core).
Axes of the slice: x: 4 (x_hi: 2, x_lo: 2; x = x_hi * 2 + x_lo), y: 4, z: 8, core: 2. Of those that a mesh axis runs over, the one named last changes fastest.
Arguments:
- inputs: bfloat16 [128, 256, 1152], P('dp', 'mp'), may hold values from -6 to 6
- cotangent: bfloat16 [128, 256, 1152], P('dp', 'mp'), may hold values from -16 to 16
- lengths: int32 [128], P('dp'), may hold values from 64 to 256
- up_weight: bfloat16 [1152, 6144], P(None, 'mp'), may hold values from -0.1875 to 0.1875
- down_weight: bfloat16 [6144, 1152], P('mp'), may hold values from -0.1875 to 0.1875
- clip_ratio: float32 [1], replicated, may hold values from 0.8 to 1.3
- count_noise: float32 [1], replicated, may hold values from -40 to 40
Outputs:
- grad_down: float32 [6144, 1152], P(('mp', 'dp'))
- ratio_next: float32 [1], replicated
All inputs are finite; a program needn't handle non-finite values.
Results may differ from a plain program's by a relative error of at most 0.0029.
Values may be sent and summed in bfloat16 or wider, within the bound.
No kernel may reach another device: no remote copies, remote signals or barrier semaphores. Data moves between devices by JAX's collectives and lax.ppermute only.
A program may use at most 128 MiB of HBM per device.

v0:
```python
import jax
import jax.numpy as jnp
from jax import lax
from jax.sharding import PartitionSpec as P

D = 1152
FF = 6144
SEQ = 256
curve_scale = 0.7978845608028654
cubic_term = 0.044715
target_share = 0.5


def gelu_parts(preact):
    cubic = preact * preact * preact
    tangent = jnp.tanh(curve_scale * (preact + cubic_term * cubic))
    values = 0.5 * preact * (1.0 + tangent)
    slopes = 0.5 * (1.0 + tangent) + 0.5 * preact * (1.0 - tangent * tangent) * curve_scale * (
        1.0 + 3.0 * cubic_term * preact * preact
    )
    return (values, slopes)


def batch_outer(left, right):
    return jnp.einsum("bsf,bsd->bfd", left, right, preferred_element_type=jnp.float32)


def batch_gram(matrix):
    return jnp.einsum("bsd,btd->bst", matrix, matrix, preferred_element_type=jnp.float32)


def per_device(inputs, cotangent, lengths, up_weight, down_weight, clip_ratio, count_noise):
    inputs_all, cotan_all = (
        lax.all_gather(inputs, "mp", axis=1, tiled=True),
        lax.all_gather(cotangent, "mp", axis=1, tiled=True),
    )
    seq_total = inputs_all.shape[1]
    positions = lax.broadcasted_iota(jnp.int32, (lengths.shape[0], seq_total), 1)
    keep = (positions < lengths[:, None]).astype(jnp.bfloat16)
    masked = cotan_all * keep[:, :, None]
    preact = jnp.einsum("bsd,df->bsf", inputs_all, up_weight, preferred_element_type=jnp.float32)
    values, slopes = gelu_parts(preact)
    hidden = values.astype(jnp.bfloat16)
    backward = jnp.einsum("bsd,fd->bsf", masked, down_weight, preferred_element_type=jnp.float32)
    delta = (backward * slopes).astype(jnp.bfloat16)
    first = jnp.sum(batch_gram(inputs_all) * batch_gram(delta), axis=(1, 2))
    second = jnp.sum(batch_gram(hidden) * batch_gram(masked), axis=(1, 2))
    partial_squares = first + second
    squares = lax.psum(partial_squares, "mp")
    norms = jnp.sqrt(squares)
    clip = clip_ratio[0] * jnp.sqrt(jnp.float32(SEQ * D * FF))
    factors = clip / jnp.maximum(norms, clip)
    examples_all = lax.axis_size("dp") * lengths.shape[0]
    soft = jax.nn.sigmoid(4.0 * (clip - norms) / clip)
    count_total = lax.psum(jnp.sum(soft), "dp")
    share = (count_total + count_noise[0]) / examples_all
    ratio_next = clip_ratio * jnp.exp(-(share - target_share))
    pieces = batch_outer(hidden, masked)
    grad_down = lax.psum_scatter(
        jnp.sum(factors[:, None, None] * pieces, axis=0) / examples_all,
        "dp",
        scatter_dimension=0,
        tiled=True,
    )
    return (grad_down, ratio_next)


def solution(mesh):
    return jax.shard_map(
        per_device,
        mesh=mesh,
        in_specs=(
            P("dp", "mp", None),
            P("dp", "mp", None),
            P("dp"),
            P(None, "mp"),
            P("mp", None),
            P(),
            P(),
        ),
        out_specs=(P(("mp", "dp"), None), P()),
        check_vma=False,
    )
```

profile of v0, /device:TPU:4, one launch (start us, length us, event | category | flops | bytes accessed | tf_op | source)
XLA Modules:
  0.0 430.4 jit_solution(10125669803366043560)
XLA Ops:
  7.2 0.0 copy-start
  7.2 0.0 all-gather.5.cloned.1.call-start
  7.2 0.7 all-gather.5.cloned.1.call-update
  7.9 0.0 all-gather.3.cloned.1.call-start
  8.0 0.7 all-gather.3.cloned.1.call-update
  8.7 0.0 reduce-scatter.5.cloned.1.call-start
  9.4 0.7 compare_convert_fusion
  10.1 24.1 %all-gather.5.cloned.1.call-done = bf16[2,256,1152]{2,1,0:T(8,128)(2,1)} async-done(((bf16[2,64,1152]{2,1,0:T(8,128)(2,1)}), bf16[2,256,1152]{2,1,0:T(8,128)(2,1)}) %all-gather.5.cloned.1.call-update) | async-done | bytes 1179664 | tf_op jit(solution)/shard_map/all_gather | solution.py:35
  34.2 3.0 fusion.21
  37.2 22.3 %all-gather.3.cloned.1.call-done = bf16[2,256,1152]{2,1,0:T(8,128)(2,1)} async-done(((bf16[2,64,1152]{2,1,0:T(8,128)(2,1)}), bf16[2,256,1152]{2,1,0:T(8,128)(2,1)}) %all-gather.3.cloned.1.call-update) | async-done | bytes 1179664 | tf_op jit(solution)/shard_map/all_gather | solution.py:34
  59.5 0.0 copy-done
  59.5 0.0 copy-start.5
  59.5 3.5 fusion.1
  63.1 0.0 copy-done.5
  63.1 0.0 copy-start.4
  63.1 0.0 copy-start.1
  63.1 0.0 copy-start.2
  63.1 0.0 copy-start.3
  63.1 2.4 fusion.19
  65.5 0.0 copy-done.1
  65.5 0.5 fusion.27
  66.0 0.0 copy-done.4
  66.0 0.5 copy-done.2
  66.6 0.3 copy-done.3
  66.9 3.6 fusion.15
  70.5 0.7 fusion.18
  71.2 10.2 %psum.14 = f32[2]{0:T(128)S(1)} all-reduce(f32[2]{0:T(128)S(1)} %add.33), channel_id=1, replica_groups=mesh['dp'=64,'mp'=4] {'mp'}, use_global_device_ids=true, to_apply=%region_2.0 | all-reduce | flops 2 | bytes 16 | tf_op jit(solution)/shard_map/psum | solution.py:49
  81.4 0.7 divide_reduce_fusion
  82.0 5.8 %fusion = f32[1536,1152]{1,0:T(8,128)S(1)} fusion(f32[2]{0:T(128)S(1)} %get-tuple-element.3, bf16[2,256,1152]{2,1,0:T(8,128)(2,1)} %all-gather.5.cloned.1.call-done, bf16[2,256]{1,0:T(2,128)(2,1)S(1)} %compare_convert_fusion, f32[2,256,1536]{2,1,0:T(8,128)} %copy-done.4), kind=kOutput, calls=%fused_computation.3 | convolution fusion | flops 1824915456 | bytes 11404296 | tf_op jit(solution)/shard_map/bsf,bsd->bfd/dot_general | solution.py:25
  87.8 3.4 broadcast_multiply_fusion
  91.2 0.0 reduce-scatter.5.cloned.1.call-update
  91.9 159.8 %psum.15 = f32[]{:T(128)} all-reduce(f32[]{:T(128)} %get-tuple-element.2), channel_id=1, replica_groups=mesh['dp'=64,'mp'=4] {'dp'}, use_global_device_ids=true, to_apply=%region_6.0 | all-reduce | flops 1 | bytes 8 | tf_op jit(solution)/shard_map/psum | solution.py:55
  252.4 170.4 %reduce-scatter.5.cloned.1.call-done = f32[24,1152]{1,0:T(8,128)} async-done(((f32[1536,1152]{1,0:T(8,128)}), f32[24,1152]{1,0:T(8,128)}) %reduce-scatter.5.cloned.1.call-update) | async-done | bytes 110608
  (1 shorter events, 0.0 us)
Async XLA Ops:
  7.2 52.4 %copy-start = (bf16[1152,1536]{1,0:T(8,128)(2,1)S(1)}, bf16[1152,1536]{1,0:T(8,128)(2,1)}, u32[]{:S(2)}) copy-start(bf16[1152,1536]{1,0:T(8,128)(2,1)} %param.10) | copy-start | bytes 10616836
  7.2 27.0 %all-gather.5.cloned.1.call-start = ((), (), s32[]{:S(2)}) async-start(), calls=%async_computation.2 | async-start | bytes 1474560 | tf_op jit(solution)/shard_map/all_gather | solution.py:35
  7.9 51.6 %all-gather.3.cloned.1.call-start = ((), (), s32[]{:S(2)}) async-start(), calls=%async_computation.1 | async-start | bytes 1474560 | tf_op jit(solution)/shard_map/all_gather | solution.py:34
  8.7 414.1 %reduce-scatter.5.cloned.1.call-start = ((), (), s32[]{:S(2)}) async-start(), calls=%async_computation.3 | async-start | bytes 7188480
  59.5 3.5 copy-start.5
  63.1 3.0 copy-start.4
  63.1 2.4 copy-start.1
  63.1 3.5 copy-start.2
  63.1 3.8 copy-start.3
Sparse Core Ops, SparseCore 0:
  9.8 24.2 all-gather.4
  36.0 23.5 all-gather.2
  91.4 331.3 reduce-scatter.4
where the time goes:
time: 431 us; the launch traced here: 430 us
  waiting for transfers between devices  218 us (51%)
  blocking collectives  170 us (39%)
  matrix products  19.5 us (5%)
  between operations  17 us (4%)
  other arithmetic  4.76 us (1%)
    unnamed x4, waiting for transfers between devices  172 us
    psum x1, blocking collectives, per_device(): count_total = lax.psum(jnp.sum(soft), 'dp')  160 us
    all_gather x1, waiting for transfers between devices, per_device(): lax.all_gather(cotangent, 'mp', axis=1, tiled=True)  24.1 us
    all_gather x1, waiting for transfers between devices, per_device(): lax.all_gather(inputs, 'mp', axis=1, tiled=True)  22.3 us
    psum x1, blocking collectives, per_device(): squares = lax.psum(partial_squares, 'mp')  10.2 us
  transfers between devices with their start and end apart: 3, of which 3 were waited for; matrix products, arithmetic and copies ran while one was open for 1% of the time, Pallas kernels for 0%

commit v1 on v0

--- a/solution.py
+++ b/solution.py
@@ -32,7 +32,9 @@
 def per_device(inputs, cotangent, lengths, up_weight, down_weight, clip_ratio, count_noise):
     inputs_all, cotan_all = (
         lax.all_gather(inputs, "mp", axis=1, tiled=True),
-        lax.all_gather(cotangent, "mp", axis=1, tiled=True),
+        jnp.concatenate(
+            lax.all_to_all(jnp.stack([cotangent] * lax.axis_size("mp")), "mp", 0, 0), axis=1
+        ),
     )
     seq_total = inputs_all.shape[1]
     positions = lax.broadcasted_iota(jnp.int32, (lengths.shape[0], seq_total), 1)

time: 431 us -> 411 us (0.954)
  waiting for transfers between devices: 218 us -> 187 us
  starting transfers between devices: 0.11 us -> 6.5 us
  local copies, waits for them, and re-layouts: 0.9 us -> 5.8 us
    all_gather x1 -> x0, waiting for transfers between devices: 24.1 us -> none  [per_device(): lax.all_gather(cotangent, 'mp', axis=1, tiled=True)]
    all_gather x1, waiting for transfers between devices: 22.3 us -> 0.01 us  [per_device(): lax.all_gather(inputs, 'mp', axis=1, tiled=True)]
    all_to_all x0 -> x1, waiting for transfers between devices: none -> 18 us  [per_device(): lax.all_to_all(jnp.stack([cotangent] * lax.axis_size('mp')), 'mp', 0, 0)]
    all_to_all x0 -> x1, starting transfers between devices: none -> 6.46 us  [per_device(): lax.all_to_all(jnp.stack([cotangent] * lax.axis_size('mp')), 'mp', 0, 0)]
    unnamed x4 -> x3, waiting for transfers between devices: 172 us -> 169 us
  transfers between devices with their start and end apart: 3 -> 3, of which waited for: 3 -> 2; matrix products, arithmetic and copies ran while one was open for 1% -> 1% of each run, Pallas kernels for 0% -> 0%
where the time goes in v1:
time: 411 us
  waiting for transfers between devices  187 us (45%)
  blocking collectives  172 us (42%)
  matrix products  17.8 us (4%)
  between operations  17.3 us (4%)
  starting transfers between devices  6.5 us (2%)
  local copies, waits for them, and re-layouts  5.8 us (1%)
  other arithmetic  4.35 us (1%)
    unnamed x3, waiting for transfers between devices  169 us
    psum x1, blocking collectives, per_device(): count_total = lax.psum(jnp.sum(soft), 'dp')  163 us
    all_to_all x1, waiting for transfers between devices, per_device(): lax.all_to_all(jnp.stack([cotangent] * lax.axis_size('mp')), 'mp', 0, 0)  18 us
    psum x1, blocking collectives, per_device(): squares = lax.psum(partial_squares, 'mp')  9.42 us
  transfers between devices with their start and end apart: 3, of which 2 were waited for; matrix products, arithmetic and copies ran while one was open for 1% of the time, Pallas kernels for 0%

profile of v1, /device:TPU:4, one launch (start us, length us, event | category | flops | bytes accessed | tf_op | source)
XLA Modules:
  0.0 411.1 jit_solution(11806227417980310562)
XLA Ops:
  7.2 0.0 copy-start
  7.2 0.0 copy-start.6
  7.2 0.0 all-gather.2.cloned.1.call-start
  7.2 0.7 all-gather.2.cloned.1.call-update
  7.9 2.3 stack.2
  10.2 6.5 %all-to-all-start = ((bf16[4,2,64,1152]{3,2,1,0:T(8,128)(2,1)}), bf16[4,2,64,1152]{3,2,1,0:T(8,128)(2,1)}, u32[]{:S(2)}, u32[]{:S(2)}) async-start(bf16[4,2,64,1152]{3,2,1,0:T(8,128)(2,1)} %stack.2), calls=%async_computation | async-start | bytes 2359296 | tf_op jit(solution)/shard_map/all_to_all | solution.py:36
  16.7 0.0 reduce-scatter.5.cloned.1.call-start
  17.3 0.0 copy-done.6
  17.4 0.1 compare_convert_fusion
  17.4 18.0 %all-to-all-done = bf16[4,2,64,1152]{3,2,1,0:T(8,128)(2,1)} async-done(((bf16[4,2,64,1152]{3,2,1,0:T(8,128)(2,1)}), bf16[4,2,64,1152]{3,2,1,0:T(8,128)(2,1)}, u32[]{:S(2)}, u32[]{:S(2)}) %all-to-all-start) | async-done | bytes 1179680 | tf_op jit(solution)/shard_map/all_to_all | solution.py:36
  35.5 1.4 copy.11
  36.8 0.2 bitcast_multiply_fusion
  37.1 0.0 copy-start.1
  37.1 1.0 copy-done.1
  38.1 1.3 fusion.21
  39.4 0.0 all-gather.2.cloned.1.call-done
  39.4 0.0 copy-done
  39.4 0.0 copy-start.4
  39.4 3.5 fusion.1
  43.0 0.0 copy-done.4
  43.0 0.0 copy-start.7
  43.0 0.0 copy-start.2
  43.0 0.0 copy-start.5
  43.0 2.4 fusion.19
  45.4 0.0 copy-done.7
  45.4 0.0 copy-done.2
  45.4 1.1 copy-done.5
  46.5 0.0 copy-start.3
  46.5 3.6 fusion.15
  50.1 0.0 copy-done.3
  50.1 0.5 fusion.20
  50.6 0.7 fusion.18
  51.3 9.4 %psum.14 = f32[2]{0:T(128)S(1)} all-reduce(f32[2]{0:T(128)S(1)} %add.33), channel_id=1, replica_groups=mesh['dp'=64,'mp'=4] {'mp'}, use_global_device_ids=true, to_apply=%region_2.0 | all-reduce | flops 2 | bytes 16 | tf_op jit(solution)/shard_map/psum | solution.py:51
  60.7 0.7 divide_reduce_fusion
  61.4 5.7 %fusion = f32[1536,1152]{1,0:T(8,128)S(1)} fusion(bf16[2,256,1152]{2,1,0:T(8,128)(2,1)} %copy-done.1, f32[2]{0:T(128)S(1)} %get-tuple-element.3, f32[2,256,1536]{2,1,0:T(8,128)} %copy-done.7), kind=kOutput, calls=%fused_computation.3 | convolution fusion | flops 1824325632 | bytes 11403272 | tf_op jit(solution)/shard_map/bsf,bsd->bfd/dot_general | solution.py:25
  67.1 3.4 broadcast_multiply_fusion
  70.5 0.0 reduce-scatter.5.cloned.1.call-update
  71.2 163.0 %psum.15 = f32[]{:T(128)} all-reduce(f32[]{:T(128)} %get-tuple-element.2), channel_id=1, replica_groups=mesh['dp'=64,'mp'=4] {'dp'}, use_global_device_ids=true, to_apply=%region_6.0 | all-reduce | flops 1 | bytes 8 | tf_op jit(solution)/shard_map/psum | solution.py:57
  234.9 168.2 %reduce-scatter.5.cloned.1.call-done = f32[24,1152]{1,0:T(8,128)} async-done(((f32[1536,1152]{1,0:T(8,128)}), f32[24,1152]{1,0:T(8,128)}) %reduce-scatter.5.cloned.1.call-update) | async-done | bytes 110608
  (1 shorter events, 0.0 us)
Async XLA Ops:
  7.2 32.3 %copy-start = (bf16[1152,1536]{1,0:T(8,128)(2,1)S(1)}, bf16[1152,1536]{1,0:T(8,128)(2,1)}, u32[]{:S(2)}) copy-start(bf16[1152,1536]{1,0:T(8,128)(2,1)} %param.10) | copy-start | bytes 10616836
  7.2 10.2 %copy-start.6 = (s32[2]{0:T(128)S(1)}, s32[2]{0:T(128)}, u32[]{:S(2)}) copy-start(s32[2]{0:T(128)} %param.9) | copy-start | bytes 28
  7.2 32.2 %all-gather.2.cloned.1.call-start = ((), (), s32[]{:S(2)}) async-start(), calls=%async_computation.2 | async-start | bytes 1474560 | tf_op jit(solution)/shard_map/all_gather | solution.py:34
  10.2 25.2 %all-to-all-start = ((bf16[4,2,64,1152]{3,2,1,0:T(8,128)(2,1)}), bf16[4,2,64,1152]{3,2,1,0:T(8,128)(2,1)}, u32[]{:S(2)}, u32[]{:S(2)}) async-start(bf16[4,2,64,1152]{3,2,1,0:T(8,128)(2,1)} %stack.2), calls=%async_computation | async-start | bytes 2359296 | tf_op jit(solution)/shard_map/all_to_all | solution.py:36
  16.7 386.4 %reduce-scatter.5.cloned.1.call-start = ((), (), s32[]{:S(2)}) async-start(), calls=%async_computation.3 | async-start | bytes 7188480
  37.1 1.0 copy-start.1
  39.4 3.5 copy-start.4
  43.0 2.4 copy-start.7
  43.0 2.4 copy-start.2
  43.0 3.5 copy-start.5
  46.5 3.6 copy-start.3
Sparse Core Ops, SparseCore 0:
  9.8 28.8 all-gather.1
  70.7 332.4 reduce-scatter.4

commit v2 on v0

--- a/solution.py
+++ b/solution.py
@@ -46,7 +46,7 @@
     first = jnp.sum(batch_gram(inputs_all) * batch_gram(delta), axis=(1, 2))
     second = jnp.sum(batch_gram(hidden) * batch_gram(masked), axis=(1, 2))
     partial_squares = first + second
-    squares = lax.psum(partial_squares, "mp")
+    squares = jnp.sum(lax.all_gather(partial_squares, "mp"), axis=0)
     norms = jnp.sqrt(squares)
     clip = clip_ratio[0] * jnp.sqrt(jnp.float32(SEQ * D * FF))
     factors = clip / jnp.maximum(norms, clip)

time: 431 us -> 431 us (level)
    psum x1 -> x0, blocking collectives: 10.2 us -> none  [per_device(): squares = lax.psum(partial_squares, 'mp')]
    unnamed x0 -> x1, blocking collectives: none -> 10.2 us
where the time goes in v2:
time: 431 us
  waiting for transfers between devices  216 us (50%)
  blocking collectives  170 us (39%)
  matrix products  19.5 us (5%)
  between operations  17.6 us (4%)
  other arithmetic  4.87 us (1%)
    unnamed x4, waiting for transfers between devices  172 us
    psum x1, blocking collectives, per_device(): count_total = lax.psum(jnp.sum(soft), 'dp')  160 us
    all_gather x1, waiting for transfers between devices, per_device(): lax.all_gather(inputs, 'mp', axis=1, tiled=True)  22.3 us
    all_gather x1, waiting for transfers between devices, per_device(): lax.all_gather(cotangent, 'mp', axis=1, tiled=True)  22.2 us
    unnamed x1, blocking collectives  10.2 us
  transfers between devices with their start and end apart: 3, of which 3 were waited for; matrix products, arithmetic and copies ran while one was open for 1% of the time, Pallas kernels for 0%

profile of v2, /device:TPU:4, one launch (start us, length us, event | category | flops | bytes accessed | tf_op | source)
XLA Modules:
  0.0 430.7 jit_solution(16658695860374701434)
XLA Ops:
  7.2 0.0 copy-start
  7.2 0.0 all-gather.6.cloned.1.call-start
  7.2 0.7 all-gather.6.cloned.1.call-update
  7.9 0.0 all-gather.4.cloned.1.call-start
  8.0 0.7 all-gather.4.cloned.1.call-update
  8.7 0.0 reduce-scatter.5.cloned.1.call-start
  9.4 1.3 dynamic-slice
  11.3 0.7 compare_convert_fusion
  12.0 22.2 %all-gather.6.cloned.1.call-done = bf16[2,256,1152]{2,1,0:T(8,128)(2,1)} async-done(((bf16[2,64,1152]{2,1,0:T(8,128)(2,1)}), bf16[2,256,1152]{2,1,0:T(8,128)(2,1)}) %all-gather.6.cloned.1.call-update) | async-done | bytes 1179664 | tf_op jit(solution)/shard_map/all_gather | solution.py:35
  34.2 3.0 fusion.21
  37.2 22.3 %all-gather.4.cloned.1.call-done = bf16[2,256,1152]{2,1,0:T(8,128)(2,1)} async-done(((bf16[2,64,1152]{2,1,0:T(8,128)(2,1)}), bf16[2,256,1152]{2,1,0:T(8,128)(2,1)}) %all-gather.4.cloned.1.call-update) | async-done | bytes 1179664 | tf_op jit(solution)/shard_map/all_gather | solution.py:34
  59.5 0.0 copy-done
  59.5 0.0 copy-start.5
  59.5 3.5 fusion.1
  63.1 0.0 copy-done.5
  63.1 0.0 copy-start.4
  63.1 0.0 copy-start.1
  63.1 0.0 copy-start.2
  63.1 0.0 copy-start.3
  63.1 2.4 fusion.19
  65.5 0.0 copy-done.1
  65.5 0.5 fusion.27
  66.0 0.0 copy-done.4
  66.0 0.5 copy-done.2
  66.6 0.3 copy-done.3
  66.9 3.6 fusion.15
  70.5 0.7 fusion.18
  71.2 0.1 add_dynamic-update-slice_fusion
  71.3 10.2 %all-reduce = f32[8]{0:T(128)S(1)} all-reduce(f32[8]{0:T(128)S(1)} %add_dynamic-update-slice_fusion), channel_id=2, replica_groups=mesh['dp'=64,'mp'=4] {'mp'}, use_global_device_ids=true, to_apply=%add | all-reduce | flops 8 | bytes 64
  81.4 0.1 reshape.43
  81.6 0.7 divide_reduce_fusion
  82.2 5.8 %fusion = f32[1536,1152]{1,0:T(8,128)S(1)} fusion(f32[2]{0:T(128)S(1)} %get-tuple-element.3, bf16[2,256,1152]{2,1,0:T(8,128)(2,1)} %all-gather.6.cloned.1.call-done, bf16[2,256]{1,0:T(2,128)(2,1)S(1)} %compare_convert_fusion, f32[2,256,1536]{2,1,0:T(8,128)} %copy-done.4), kind=kOutput, calls=%fused_computation.3 | convolution fusion | flops 1824915456 | bytes 11404296 | tf_op jit(solution)/shard_map/bsf,bsd->bfd/dot_general | solution.py:25
  88.0 3.4 broadcast_multiply_fusion
  91.4 0.0 reduce-scatter.5.cloned.1.call-update
  92.1 159.7 %psum.7 = f32[]{:T(128)} all-reduce(f32[]{:T(128)} %get-tuple-element.2), channel_id=1, replica_groups=mesh['dp'=64,'mp'=4] {'dp'}, use_global_device_ids=true, to_apply=%region_6.0 | all-reduce | flops 1 | bytes 8 | tf_op jit(solution)/shard_map/psum | solution.py:55
  252.4 170.6 %reduce-scatter.5.cloned.1.call-done = f32[24,1152]{1,0:T(8,128)} async-done(((f32[1536,1152]{1,0:T(8,128)}), f32[24,1152]{1,0:T(8,128)}) %reduce-scatter.5.cloned.1.call-update) | async-done | bytes 110608
  (2 shorter events, 0.0 us)
Async XLA Ops:
  7.2 52.4 %copy-start = (bf16[1152,1536]{1,0:T(8,128)(2,1)S(1)}, bf16[1152,1536]{1,0:T(8,128)(2,1)}, u32[]{:S(2)}) copy-start(bf16[1152,1536]{1,0:T(8,128)(2,1)} %param.10) | copy-start | bytes 10616836
  7.2 27.0 %all-gather.6.cloned.1.call-start = ((), (), s32[]{:S(2)}) async-start(), calls=%async_computation.2 | async-start | bytes 1474560 | tf_op jit(solution)/shard_map/all_gather | solution.py:35
  7.9 51.6 %all-gather.4.cloned.1.call-start = ((), (), s32[]{:S(2)}) async-start(), calls=%async_computation.1 | async-start | bytes 1474560 | tf_op jit(solution)/shard_map/all_gather | solution.py:34
  8.7 414.4 %reduce-scatter.5.cloned.1.call-start = ((), (), s32[]{:S(2)}) async-start(), calls=%async_computation.3 | async-start | bytes 7188480
  59.5 3.5 copy-start.5
  63.1 3.0 copy-start.4
  63.1 2.4 copy-start.1
  63.1 3.5 copy-start.2
  63.1 3.8 copy-start.3
Sparse Core Ops, SparseCore 0:
  9.8 24.2 all-gather.5
  36.0 23.5 all-gather.3
  91.6 331.4 reduce-scatter.4
